TPU v7x, 128 devices: a whole 4x4x4 slice. The times are simulated.
128 devices in a mesh: row: 8 (over x, y_hi), col: 16 (over y_lo, z, core).
Axes of the slice: x: 4, y: 4 (y_hi: 2, y_lo: 2; y = y_hi * 2 + y_lo), z: 4, core: 2. Of those that a mesh axis runs over, the one named last changes fastest.
Arguments:
- queries: float32 [2, 384, 20480], P(None, 'col', 'row'), may hold values from -6 to 6
- precond: float32 [20480, 20480], P('row', 'col'), may hold values from -0.0390625 to 0.0390625
- column_gain: float32 [20480], P('col'), may hold values from 0.5 to 2
- store: bfloat16 [24576, 20480], P('row', 'col'), may hold values from -0.0390625 to 0.0390625
Outputs:
- scores: float32 [2, 384, 24576], P(None, 'col', 'row')
All inputs are finite; a program needn't handle non-finite values.
Results may differ from a plain program's by a relative error of at most 0.0029.
Values sent between devices are 32-bit elements; how exact they have to be, the bound alone decides.
A program may use at most 128 MiB of HBM per device.

v0:
```python
import jax
import jax.numpy as jnp
from jax import lax
from jax.sharding import PartitionSpec as P


def score_block(lowered, store):
    return lax.dot_general(
        lowered, store, (((1,), (1,)), ((), ())), preferred_element_type=jnp.float32
    )


def local(queries, precond, column_gain, store):
    own_rows = queries.shape[1]
    results = []
    for batch_index in range(queries.shape[0]):
        local_rows = queries[batch_index]
        partial_rows = jnp.dot(
            lax.all_gather(local_rows, "col", axis=0, tiled=True),
            precond,
            precision=lax.Precision.HIGHEST,
            preferred_element_type=jnp.float32,
        )
        summed = lax.psum(partial_rows, "row")
        lowered = (summed * column_gain[None, :]).astype(jnp.bfloat16)
        whole_sum = lax.psum(score_block(lowered, store), "col")
        own_scores = lax.dynamic_slice_in_dim(
            whole_sum, lax.axis_index("col") * own_rows, own_rows, 0
        )
        results.append(own_scores)
    return jnp.stack(results)


def solution(mesh):
    return jax.shard_map(
        local,
        mesh=mesh,
        in_specs=(P(None, "col", "row"), P("row", "col"), P("col"), P("row", "col")),
        out_specs=P(None, "col", "row"),
        check_vma=False,
    )
```

profile of v0, /device:TPU:1, one launch (start us, length us, event | category | flops | bytes accessed | tf_op | source)
XLA Modules:
  0.0 461.2 jit_solution(7447475369689658394)
XLA Ops:
  6.5 0.0 all-gather.7.cloned.1.call-start
  6.5 1.9 fusion.8
  8.4 0.0 all-gather.7.cloned.1.call-update
  8.4 0.0 all-gather.5.cloned.1.call-start
  8.5 0.7 all-gather.5.cloned.1.call-update
  9.2 0.0 all-reduce.7.cloned.1.call-start
  9.2 40.7 %all-gather.7.cloned.1.call-done = f32[1,384,2560]{2,1,0:T(8,128)} async-done(((f32[1,24,2560]{2,1,0:T(8,128)}), f32[1,384,2560]{2,1,0:T(8,128)}) %all-gather.7.cloned.1.call-update) | async-done | bytes 3932176 | tf_op jit(solution)/shard_map/all_gather | solution.py:19
  49.9 21.0 %fusion = f32[384,1280]{1,0:T(8,128)} fusion(f32[2560,1280]{1,0:T(8,128)} %param.5, f32[1,384,2560]{2,1,0:T(8,128)} %all-gather.7.cloned.1.call-done), kind=kOutput, calls=%fused_computation | convolution fusion | flops 15099494400 | bytes 19005440 | tf_op jit(solution)/shard_map/dot_general | solution.py:18
  70.9 0.0 copy-start.1
  70.9 17.8 %all-gather.5.cloned.1.call-done = f32[1,384,2560]{2,1,0:T(8,128)} async-done(((f32[1,24,2560]{2,1,0:T(8,128)}), f32[1,384,2560]{2,1,0:T(8,128)}) %all-gather.5.cloned.1.call-update) | async-done | bytes 3932176 | tf_op jit(solution)/shard_map/all_gather | solution.py:19
  88.7 21.1 %fusion.2 = f32[384,1280]{1,0:T(8,128)} fusion(f32[2560,1280]{1,0:T(8,128)} %param.5, f32[1,384,2560]{2,1,0:T(8,128)} %all-gather.5.cloned.1.call-done), kind=kOutput, calls=%fused_computation.2 | convolution fusion | flops 15099494400 | bytes 19005440 | tf_op jit(solution)/shard_map/dot_general | solution.py:18
  109.8 0.0 all-reduce.7.cloned.1.call-update
  109.8 0.0 all-reduce.5.cloned.1.call-start
  109.9 176.0 %all-reduce.7.cloned.1.call-done = (f32[384,1280]{1,0:T(8,128)}, f32[384,1280]{1,0:T(8,128)}) async-done(((f32[384,1280]{1,0:T(8,128)}, f32[384,1280]{1,0:T(8,128)}), (f32[384,1280]{1,0:T(8,128)}, f32[384,1280]{1,0:T(8,128)})) %all-reduce.7.cloned.1.call-update) | async-done | bytes 3932176 | tf_op jit(solution)/shard_map/psum | solution.py:24
  285.9 0.0 copy-done.1
  285.9 0.0 copy-start
  285.9 9.3 %fusion.4 = f32[384,3072]{1,0:T(8,128)} fusion(bf16[3072,1280]{1,0:T(8,128)(2,1)} %param.7, f32[384,1280]{1,0:T(8,128)} %get-tuple-element.8, f32[1280]{0:T(1024)S(1)} %copy-done.1), kind=kOutput, calls=%fused_computation.6 | convolution fusion | flops 3020881920 | bytes 14554112 | tf_op jit(solution)/shard_map/dot_general | solution.py:8
  295.2 0.0 copy-done
  295.2 10.0 %fusion.5 = f32[384,3072]{1,0:T(8,128)} fusion(bf16[3072,1280]{1,0:T(8,128)(2,1)} %param.7, f32[384,1280]{1,0:T(8,128)S(1)} %copy-done, f32[1280]{0:T(1024)S(1)} %copy-done.1), kind=kOutput, calls=%fused_computation.7 | convolution fusion | flops 3020881920 | bytes 14554112 | tf_op jit(solution)/shard_map/dot_general | solution.py:8
  305.3 0.0 all-reduce.5.cloned.1.call-update
  305.3 147.4 %all-reduce.5.cloned.1.call-done = (f32[384,3072]{1,0:T(8,128)}, f32[384,3072]{1,0:T(8,128)}) async-done(((f32[384,3072]{1,0:T(8,128)}, f32[384,3072]{1,0:T(8,128)}), (f32[384,3072]{1,0:T(8,128)}, f32[384,3072]{1,0:T(8,128)})) %all-reduce.5.cloned.1.call-update) | async-done | bytes 9437200 | tf_op jit(solution)/shard_map/psum | solution.py:26
  452.7 1.1 dynamic-slice_bitcast_fusion
  453.8 0.9 pad_maximum_fusion
Async XLA Ops:
  6.5 43.4 %all-gather.7.cloned.1.call-start = ((), (), s32[]{:S(2)}) async-start(), calls=%async_computation.1 | async-start | bytes 4177920 | tf_op jit(solution)/shard_map/all_gather | solution.py:19
  8.4 80.3 %all-gather.5.cloned.1.call-start = ((), (), s32[]{:S(2)}) async-start(), calls=%async_computation | async-start | bytes 4177920 | tf_op jit(solution)/shard_map/all_gather | solution.py:19
  9.2 276.7 %all-reduce.7.cloned.1.call-start = ((), (), s32[]{:S(2)}) async-start(), calls=%async_computation.3 | async-start | bytes 7864320 | tf_op jit(solution)/shard_map/psum | solution.py:24
  70.9 215.0 %copy-start.1 = (f32[1280]{0:T(1024)S(1)}, f32[1280]{0:T(1024)}, u32[]{:S(2)}) copy-start(f32[1280]{0:T(1024)} %param.6) | copy-start | bytes 15364
  109.8 342.8 %all-reduce.5.cloned.1.call-start = ((), (), s32[]{:S(2)}) async-start(), calls=%async_computation.2 | async-start | bytes 18874368 | tf_op jit(solution)/shard_map/psum | solution.py:26
  285.9 9.3 %copy-start = (f32[384,1280]{1,0:T(8,128)S(1)}, f32[384,1280]{1,0:T(8,128)}, u32[]{:S(2)}) copy-start(f32[384,1280]{1,0:T(8,128)} %get-tuple-element.7) | copy-start | bytes 5898244
Sparse Core Ops, SparseCore 0:
  9.1 40.8 all-gather.6
  51.6 37.0 all-gather.4
  109.9 175.9 all-reduce.6
  305.4 147.2 all-reduce.4
where the time goes:
time: 462 us; the launch traced here: 461 us
  waiting for transfers between devices  383 us (83%)
  matrix products  61.4 us (13%)
  between operations  13.1 us (3%)
    psum x1, waiting for transfers between devices, local(): summed = lax.psum(partial_rows, 'row')  176 us
    psum x1, waiting for transfers between devices, local(): whole_sum = lax.psum(score_block(lowered, store), 'col')  147 us
    all_gather x2, waiting for transfers between devices, local(): lax.all_gather(local_rows, 'col', axis=0, tiled=True)  58.5 us
    dot_general x2, matrix products, local(): jnp.dot(lax.all_gather(local_rows, 'col', axis=0, tiled=True), precond, p...  42.1 us
    dot_general x2, matrix products, score_block(): lax.dot_general(lowered, store, (((1,), (1,)), ((), ())), preferred_eleme...  19.4 us
  transfers between devices with their start and end apart: 4, of which 4 were waited for; matrix products, arithmetic and copies ran while one was open for 5% of the time, Pallas kernels for 0%

commit v1 on v0

v1 whole, which is shorter than its diff:
```python
import functools

import jax
import jax.numpy as jnp
from jax import lax
from jax.experimental import pallas as pl
from jax.experimental.pallas import tpu as pltpu
from jax.sharding import PartitionSpec as P

MESH = pl.DeviceIdType.MESH
Q = 8
PT = 128
F32, BF16 = jnp.float32, jnp.bfloat16


def kernel(
    n, qin, gain, precond, store, out,
    qg, qs, phi, plo, stage, p1, rx, ty, ry, low, lowb, sv, p2, rc, rz, tc, rl,
    pt_sem, st_sem, a_s, az_r, ay_r, ac_r, b_s, bx_r, by_r, bh_r, bg_r, c_s, cc_r, cz_r, cy_r,
):
    q = Q
    K, N1, N2 = phi.shape[0], phi.shape[1], sv.shape[0]
    row, col = lax.axis_index("row"), lax.axis_index("col")
    x, yh = row // 2, lax.rem(row, 2)
    yl, z, c = col // 8, lax.rem(col // 2, 4), lax.rem(col, 2)

    def dev(x=x, yh=yh, yl=yl, z=z, c=c):
        return (x * 2 + yh, yl * 8 + z * 2 + c)

    def mod4(v):
        return lax.rem(v + 4, 4)

    xn = [dev(x=mod4(x + d)) for d in (1, 2, 3)]
    zn = [dev(z=mod4(z + d)) for d in (1, 2, 3)]
    yln, yhn, cn = dev(yl=1 - yl), dev(yh=1 - yh), dev(c=1 - c)

    def rows(start, size):
        return pl.ds(pl.multiple_of(start, q), size)

    def slot(c, yl, z):
        return ((c * 2 + yl) * 4 + z) * q

    mine = rows(slot(c, yl, z), q)

    def rcopy(src, dst, ssem, rsem, device):
        return pltpu.make_async_remote_copy(
            src_ref=src, dst_ref=dst, send_sem=ssem, recv_sem=rsem, device_id=device, device_id_type=MESH
        )

    def a_z(k, d):
        return rcopy(qin.at[rows(k * q, q)], qg.at[k, mine], a_s.at[k, d - 1], az_r.at[k, d - 1], zn[d - 1])

    def a_z_in(k, d):
        there = qg.at[k, rows(slot(c, yl, mod4(z - d)), q)]
        return rcopy(there, there, a_s.at[k, d - 1], az_r.at[k, d - 1], zn[d - 1])

    def a_y(k):
        return rcopy(qin.at[rows(k * q, q)], qg.at[k, mine], a_s.at[k, 3], ay_r.at[k], yln)

    def a_yf(k, d):
        there = qg.at[k, rows(slot(c, yl, mod4(z - d)), q)]
        return rcopy(there, there, a_s.at[k, 3 + d], ay_r.at[k], yln)

    def a_y_in(k):
        there = qg.at[k, rows(slot(c, 1 - yl, 0), 4 * q)]
        return rcopy(there, there, a_s.at[k, 3], ay_r.at[k], yln)

    def a_c(k, i):
        there = qg.at[k, rows(slot(c, yl if i == 0 else 1 - yl, 0), 4 * q)]
        return rcopy(there, there, a_s.at[k, 7 + i], ac_r.at[k], cn)

    def a_c_in(k):
        there = qg.at[k, rows(slot(1 - c, 0, 0), 8 * q)]
        return rcopy(there, there, a_s.at[k, 7], ac_r.at[k], cn)

    def b_x(k, d):
        src = p1.at[lax.rem(k, 2), rows(mod4(x + d) * 4 * q, 4 * q)]
        return rcopy(src, rx.at[k, d - 1], b_s.at[k, d - 1], bx_r.at[k, d - 1], xn[d - 1])

    def b_y(k):
        return rcopy(ty.at[k], ry.at[k], b_s.at[k, 3], by_r.at[k], yhn)

    def lrows(x, yh):
        return rows(x * 4 * q + yh * 2 * q, 2 * q)

    def b_g(k, d):
        there = low.at[k, lrows(x, yh)]
        return rcopy(there, there, b_s.at[k, 3 + d], bg_r.at[k, d - 1], xn[d - 1])

    def b_h(k):
        there = low.at[k, lrows(x, yh)]
        return rcopy(there, there, b_s.at[k, 7], bh_r.at[k], yhn)

    def b_h_in(k):
        there = low.at[k, lrows(x, 1 - yh)]
        return rcopy(there, there, b_s.at[k, 7], bh_r.at[k], yhn)

    def b_gf(k, d):
        there = low.at[k, lrows(x, 1 - yh)]
        return rcopy(there, there, b_s.at[k, 7 + d], bg_r.at[k, d - 1], xn[d - 1])

    def b_g_in(k, d):
        there = low.at[k, rows(mod4(x - d) * 4 * q, 4 * q)]
        return rcopy(there, there, b_s.at[k, 3 + d], bg_r.at[k, d - 1], xn[d - 1])

    def c_c(k):
        src = p2.at[lax.rem(k, 2), rows(slot(1 - c, 0, 0), 8 * q)]
        return rcopy(src, rc.at[k], c_s.at[k, 0], cc_r.at[k], cn)

    def c_z(k, d, l):
        src = p2.at[lax.rem(k, 2), rows(slot(c, l, mod4(z + d)), q)]
        return rcopy(src, rz.at[k, d - 1, l], c_s.at[k, 2 * d - 1 + l], cz_r.at[k, d - 1], zn[d - 1])

    def c_z_in(k, d):
        there = rz.at[k, d - 1]
        return rcopy(there, there, c_s.at[k, 2 * d - 1], cz_r.at[k, d - 1], zn[d - 1])

    def c_y(k):
        return rcopy(tc.at[k], rl.at[k], c_s.at[k, 7], cy_r.at[k], yln)

    def A1(k):
        qg[k, mine] = qin[rows(k * q, q)]
        for d in (1, 3, 2):
            a_z(k, d).start()
        a_y(k).start()

    def A2(k):
        for d in (1, 3, 2):
            a_z_in(k, d).wait_recv()
            a_yf(k, d).start()
        a_c(k, 0).start()

    def A3(k):
        a_y_in(k).wait_recv()
        a_c(k, 1).start()

    def M1(k):
        a_c_in(k).wait_recv()

        @pl.when(k >= 2)
        def _():
            for d in (1, 2, 3):
                b_x(k - 2, d).wait_send()

        def split(i, _):
            part = rows(i * 16, 16)
            v = qg[k, part]
            hi = v.astype(BF16)
            qs[part] = hi
            qs[rows(16 * q + i * 16, 16)] = (v - hi.astype(F32)).astype(BF16)
            return 0

        lax.fori_loop(0, q, split, 0)

        def tile(j, _):
            cols = pl.ds(pl.multiple_of(j * 256, 256), 256)
            both = jnp.dot(qs[...], phi[:, cols], preferred_element_type=F32)
            third = jnp.dot(qs[: 16 * q], plo[:, cols], preferred_element_type=F32)
            p1[lax.rem(k, 2), :, cols] = both[: 16 * q] + (both[16 * q :] + third)
            return 0

        lax.fori_loop(0, N1 // 256, tile, 0)
        for d in (2, 1, 3):
            b_x(k, d).start()

    def B2(k):
        for d in (1, 2, 3):
            b_x(k, d).wait_recv()
        at = x * 4 * q

        def total(h):
            own = p1[lax.rem(k, 2), rows(at + h * 2 * q, 2 * q)]
            part = rows(h * 2 * q, 2 * q)
            return (own + rx[k, 0, part]) + (rx[k, 1, part] + rx[k, 2, part])

        ty[k] = total(1 - yh)
        b_y(k).start()
        low[k, lrows(x, yh)] = total(yh)

    def B3(k):
        b_y(k).wait_recv()
        here = lrows(x, yh)
        v = (low[k, here] + ry[k]) * gain[...]
        low[k, here] = v.astype(BF16).astype(F32)
        b_h(k).start()
        for d in (2, 1, 3):
            b_g(k, d).start()

    def B5(k):
        b_h_in(k).wait_recv()
        for d in (2, 1, 3):
            b_gf(k, d).start()

    def M2(k):
        for d in (1, 2, 3):
            b_g_in(k, d).wait_recv()

        @pl.when(k >= 2)
        def _():
            c_c(k - 2).wait_send()
            for d in (1, 2, 3):
                for l in (0, 1):
                    c_z(k - 2, d, l).wait_send()

        lowb[...] = low[k].astype(BF16)

        def tile(j, _):
            cols = pl.ds(pl.multiple_of(j * 256, 256), 256)
            p2[lax.rem(k, 2), :, cols] = lax.dot_general(
                lowb[...], sv[cols, :], (((1,), (1,)), ((), ())), preferred_element_type=F32
            )
            return 0

        lax.fori_loop(0, N2 // 256, tile, 0)
        c_c(k).start()

    def C1(k):
        c_c(k).wait_recv()
        here = rows(slot(c, 0, 0), 8 * q)
        p2[lax.rem(k, 2), here] = p2[lax.rem(k, 2), here] + rc[k]
        for d in (2, 1, 3):
            for l in (0, 1):
                c_z(k, d, l).start()

    def C2(k):
        for d in (1, 2, 3):
            c_z_in(k, d).wait_recv()

        def total(l):
            own = p2[lax.rem(k, 2), rows(slot(c, l, z), q)]
            return (own + rz[k, 0, l]) + (rz[k, 1, l] + rz[k, 2, l])

        tc[k] = total(1 - yl)
        c_y(k).start()
        out[rows(k * q, q)] = total(yl)

    def C3(k):
        c_y(k).wait_recv()
        out[rows(k * q, q)] = out[rows(k * q, q)] + rl[k]

    barrier = pltpu.get_barrier_semaphore()
    for peer in xn + zn + [yln, yhn, cn]:
        pl.semaphore_signal(barrier, inc=1, device_id=peer, device_id_type=MESH)

    def p_in(i):
        return pltpu.make_async_copy(
            precond.at[pl.ds(pl.multiple_of(i * PT, PT), PT)], stage.at[lax.rem(i, 2)], pt_sem.at[lax.rem(i, 2)]
        )

    p_in(0).start()
    p_in(1).start()
    s_in = pltpu.make_async_copy(store, sv, st_sem)
    pl.semaphore_wait(barrier, 9)
    A1(0)

    def split_p(i, _):
        p_in(i).wait()
        part = pl.ds(pl.multiple_of(i * PT, PT), PT)
        v = stage[lax.rem(i, 2)]
        hi = v.astype(BF16)
        phi[part] = hi
        plo[part] = (v - hi.astype(F32)).astype(BF16)

        @pl.when(i + 2 < K // PT)
        def _():
            p_in(i + 2).start()

        return 0

    half = K // PT // 2
    lax.fori_loop(0, half, split_p, 0)
    A2(0)
    A1(1)
    lax.fori_loop(half, K // PT, split_p, 0)
    s_in.start()
    A3(0)
    s_in.wait()

    def step(s, _):
        def at(task, k):
            @pl.when((k >= 0) & (k < n))
            def _():
                task(k)

        at(M1, s)
        at(A1, s + 2)
        at(A2, s + 1)
        at(B2, s - 1)
        at(C2, s - 3)
        at(M2, s - 2)
        at(B3, s - 1)
        at(C1, s - 2)
        at(B5, s - 1)
        at(A3, s + 1)
        at(C3, s - 3)
        return 0

    lax.fori_loop(0, n + 3, step, 0)

    def drain(k, _):
        for d in (1, 2, 3):
            a_z(k, d).wait_send()
            a_yf(k, d).wait_send()
            b_g(k, d).wait_send()
            b_gf(k, d).wait_send()
        a_y(k).wait_send()
        a_c(k, 0).wait_send()
        a_c(k, 1).wait_send()
        b_y(k).wait_send()
        b_h(k).wait_send()
        c_y(k).wait_send()

        @pl.when(k >= n - 2)
        def _():
            c_c(k).wait_send()
            for d in (1, 2, 3):
                b_x(k, d).wait_send()
                for l in (0, 1):
                    c_z(k, d, l).wait_send()

        return 0

    lax.fori_loop(0, n, drain, 0)


def local(queries, precond, column_gain, store):
    b, own, K = queries.shape
    q, N1, N2 = Q, precond.shape[1], store.shape[0]
    n = b * own // q
    vm = pltpu.VMEM
    dma = pltpu.SemaphoreType.DMA
    out = pl.pallas_call(
        functools.partial(kernel, n),
        out_shape=jax.ShapeDtypeStruct((b * own, N2), F32),
        in_specs=[
            pl.BlockSpec(memory_space=pltpu.VMEM),
            pl.BlockSpec(memory_space=pltpu.VMEM),
            pl.BlockSpec(memory_space=pl.ANY),
            pl.BlockSpec(memory_space=pl.ANY),
        ],
        out_specs=pl.BlockSpec(memory_space=pltpu.VMEM),
        scratch_shapes=[
            vm((n, 16 * q, K), F32),
            vm((32 * q, K), BF16),
            vm((K, N1), BF16),
            vm((K, N1), BF16),
            vm((2, PT, N1), F32),
            vm((2, 16 * q, N1), F32),
            vm((n, 3, 4 * q, N1), F32),
            vm((n, 2 * q, N1), F32),
            vm((n, 2 * q, N1), F32),
            vm((n, 16 * q, N1), F32),
            vm((16 * q, N1), BF16),
            vm((N2, N1), BF16),
            vm((2, 16 * q, N2), F32),
            vm((n, 8 * q, N2), F32),
            vm((n, 3, 2, q, N2), F32),
            vm((n, q, N2), F32),
            vm((n, q, N2), F32),
            dma((2,)),
            dma,
            dma((n, 9)),
            dma((n, 3)),
            dma((n,)),
            dma((n,)),
            dma((n, 11)),
            dma((n, 3)),
            dma((n,)),
            dma((n,)),
            dma((n, 3)),
            dma((n, 8)),
            dma((n,)),
            dma((n, 3)),
            dma((n,)),
        ],
        compiler_params=pltpu.CompilerParams(
            collective_id=0, has_side_effects=True, vmem_limit_bytes=63 * 1024 * 1024
        ),
        cost_estimate=pl.CostEstimate(flops=2 * 16 * b * own * (3 * K * N1 + N1 * N2), bytes_accessed=24 << 20, transcendentals=0),
        name="scores",
    )(queries.reshape(b * own, K), column_gain.reshape(1, N1), precond, store)
    return out.reshape(b, own, N2)


def solution(mesh):
    return jax.shard_map(
        local,
        mesh=mesh,
        in_specs=(P(None, "col", "row"), P("row", "col"), P("col"), P("row", "col")),
        out_specs=P(None, "col", "row"),
        check_vma=False,
    )
```

time: 462 us -> 187 us (0.40)
  waiting for transfers between devices: 383 us -> 0 us
  Pallas kernels: 0 us -> 183 us
  matrix products: 61.4 us -> 0 us
  between operations: 13.1 us -> 0.01 us
    psum x2 -> x0, waiting for transfers between devices: 323 us -> none  [the longest x1 176 us: local(): summed = lax.psum(partial_rows, 'row')]
    pallas_call x0 -> x1, Pallas kernels: none -> 183 us  [local(): pl.pallas_call(functools.partial(kernel, n), out_shape=jax.ShapeDtypeStru...]
    dot_general x4 -> x0, matrix products: 61.4 us -> none  [the longest x2 42.1 us: local(): jnp.dot(lax.all_gather(local_rows, 'col', axis=0, tiled=True), precond, p...]
    all_gather x2 -> x0, waiting for transfers between devices: 58.5 us -> none  [local(): lax.all_gather(local_rows, 'col', axis=0, tiled=True)]
  transfers between devices with their start and end apart: 4 -> 0, of which waited for: 4 -> 0; matrix products, arithmetic and copies ran while one was open for 5% -> 0% of each run, Pallas kernels for 0% -> 0%
where the time goes in v1:
time: 187 us; the launch traced here: 186 us
  Pallas kernels  183 us (98%)
  local copies, waits for them, and re-layouts  3.21 us (2%)
    pallas_call x1, Pallas kernels, local(): pl.pallas_call(functools.partial(kernel, n), out_shape=jax.ShapeDtypeStru...  183 us

profile of v1, /device:TPU:1, one launch (start us, length us, event | category | flops | bytes accessed | tf_op | source)
XLA Modules:
  0.0 186.2 jit_solution(8538193016138463564)
XLA Ops:
  0.0 1.3 reshape.10.gain
  1.3 183.0 %scores.1 = f32[48,3072]{1,0:T(8,128)} custom-call(f32[48,2560]{1,0:T(8,128)} %bitcast.3, f32[1,1280]{1,0:T(1,128)} %reshape.10.gain, f32[2560,1280]{1,0:T(8,128)} %precond.1, bf16[3072,1280]{1,0:T(8,128)(2,1)} %store.1), custom_call_target="tpu_custom_call" | custom-call | flops 21139292160 | bytes 25165824 | tf_op jit(solution)/shard_map/scores/pallas_call | solution.py:332
  184.3 1.9 %copy.6 = f32[2,24,3072]{2,1,0:T(8,128)} copy(f32[2,24,3072]{2,1,0:T(8,128)} %bitcast.2) | data formatting | bytes 1179648

commit v2 on v1

v2 whole, which is shorter than its diff:
```python
import functools

import jax
import jax.numpy as jnp
from jax import lax
from jax.experimental import pallas as pl
from jax.experimental.pallas import tpu as pltpu
from jax.sharding import PartitionSpec as P

MESH = pl.DeviceIdType.MESH
Q = 8
PT, NB = 128, 4
S1, S2 = 3, 3
T1, T2 = 1280, 1024
ORDER = (
    ("A1", 0), ("A1", 1), ("PR", 0), ("PR", 1), ("A2y", 0), ("A2y", 1), ("A2z", 0), ("A2c", 0), ("ST", 0),
    ("A2z", 1), ("A2c", 1), ("ST", 1), ("ST", 2), ("A3", 0), ("A1", 2), ("A3", 1), ("A1", 3), ("M1", 0),
    ("A2y", 2), ("A2y", 3), ("M1", 1), ("B1y", 0), ("A2z", 2), ("A2c", 2), ("A2z", 3), ("A2c", 3), ("B2", 0),
    ("B1y", 1), ("B2", 1), ("A3", 2), ("A3", 3), ("A1", 4), ("B3", 0), ("A1", 5), ("B3", 1), ("M1", 2),
    ("M1", 3), ("B5", 0), ("B6a", 0), ("A2y", 4), ("B5", 1), ("B6a", 1), ("A2z", 4), ("A2c", 4), ("A2y", 5),
    ("A2z", 5), ("A2c", 5), ("B1y", 2), ("B1y", 3), ("M2", 0), ("B2", 2), ("A3", 4), ("A3", 5), ("M2", 1),
    ("B2", 3), ("B3", 2), ("M1", 4), ("C1", 0), ("C1", 1), ("B5", 2), ("B3", 3), ("B6a", 2), ("M1", 5),
    ("B1y", 4), ("B6a", 3), ("C1y", 0), ("C2", 0), ("B5", 3), ("M2", 2), ("C1y", 1), ("C2", 1), ("B2", 4),
    ("B1y", 5), ("C1", 2), ("C3", 0), ("B2", 5), ("M2", 3), ("B3", 4), ("C3", 1), ("C1", 3), ("B3", 5),
    ("C1y", 2), ("C2", 2), ("B6a", 4), ("B5", 4), ("B6a", 5), ("C1y", 3), ("C2", 3), ("B5", 5), ("M2", 4),
    ("C3", 2), ("M2", 5), ("C3", 3), ("C1", 4), ("C1", 5), ("C1y", 4), ("C1y", 5), ("C2", 4), ("C3", 4),
    ("C2", 5), ("C3", 5),
)
F32, BF16 = jnp.float32, jnp.bfloat16


def kernel(
    n, qin, gain, precond, store, out,
    qg, qs, phi, plo, stage, p1, rx, rx2, ry, low, lowb, sv, sst, p2, rc, rz, rz2, rl,
    pt_sem, st_sem, a_s, az_r, azf_r, ay_r, ac_r, b_s, bx_r, by_r, bh_r, bg_r, bgf_r, c_s, cc_r, cz_r, cz2_r, cy_r,
):
    q = Q
    K, N1, N2 = phi.shape[0], phi.shape[1], sv.shape[1]
    row, col = lax.axis_index("row"), lax.axis_index("col")
    x, yh = row // 2, lax.rem(row, 2)
    yl, z, c = col // 8, lax.rem(col // 2, 4), lax.rem(col, 2)

    def dev(x=x, yh=yh, yl=yl, z=z, c=c):
        return (x * 2 + yh, yl * 8 + z * 2 + c)

    def mod4(v):
        return lax.rem(v + 4, 4)

    xn = [dev(x=mod4(x + d)) for d in (1, 2, 3)]
    zn = [dev(z=mod4(z + d)) for d in (1, 2, 3)]
    yln, yhn, cn = dev(yl=1 - yl), dev(yh=1 - yh), dev(c=1 - c)

    def rows(start, size):
        return pl.ds(pl.multiple_of(start, q), size)

    def slot(c, yl, z):
        return ((c * 2 + yl) * 4 + z) * q

    mine = rows(slot(c, yl, z), q)

    def rcopy(src, dst, ssem, rsem, device):
        return pltpu.make_async_remote_copy(
            src_ref=src, dst_ref=dst, send_sem=ssem, recv_sem=rsem, device_id=device, device_id_type=MESH
        )

    def at_slot(k, c, l, zz, count=1):
        return qg.at[k, rows(slot(c, l, zz), count * q)]

    def same(there, ssem, rsem, device):
        return rcopy(there, there, ssem, rsem, device)

    def own(k):
        return qin.at[rows(k * q, q)]

    def a_z(k, d):
        return rcopy(own(k), qg.at[k, mine], a_s.at[k, d - 1], az_r.at[k, d - 1], zn[d - 1])

    def a_z_in(k, d):
        return same(at_slot(k, c, yl, mod4(z - d)), a_s.at[k, d - 1], az_r.at[k, d - 1], zn[d - 1])

    def a_y(k):
        return rcopy(own(k), qg.at[k, mine], a_s.at[k, 3], ay_r.at[k, 0], yln)

    def a_y_in(k):
        return same(at_slot(k, c, 1 - yl, z), a_s.at[k, 3], ay_r.at[k, 0], yln)

    def a_zf(k, d):
        return same(at_slot(k, c, 1 - yl, z), a_s.at[k, 3 + d], azf_r.at[k, d - 1], zn[d - 1])

    def a_zf_in(k, d):
        return same(at_slot(k, c, 1 - yl, mod4(z - d)), a_s.at[k, 3 + d], azf_r.at[k, d - 1], zn[d - 1])

    def a_yf(k):
        return same(at_slot(k, c, yl, mod4(z + 2)), a_s.at[k, 5], ay_r.at[k, 1], yln)

    def a_yf_in(k):
        return same(at_slot(k, c, 1 - yl, mod4(z + 2)), a_s.at[k, 5], ay_r.at[k, 1], yln)

    def a_c(k, i):
        return same(at_slot(k, c, yl if i == 0 else 1 - yl, 0, 4), a_s.at[k, 7 + i], ac_r.at[k, i], cn)

    def a_c_in(k, i):
        return same(at_slot(k, 1 - c, yl if i == 0 else 1 - yl, 0, 4), a_s.at[k, 7 + i], ac_r.at[k, i], cn)

    def lrows(x, yh):
        return rows(x * 4 * q + yh * 2 * q, 2 * q)

    x2 = mod4(x + 2)
    z2 = mod4(z + 2)

    def b_y1(k):
        return rcopy(p1.at[k % S1, lrows(x2, 1 - yh)], ry.at[k, 0], b_s.at[k, 0], by_r.at[k, 0], yhn)

    def b_x(k, d):
        src = p1.at[k % S1, rows(mod4(x + d) * 4 * q, 4 * q)]
        return rcopy(src, rx.at[k, d // 2], b_s.at[k, d], bx_r.at[k, d - 1], xn[d - 1])

    def b_x2(k):
        return rcopy(ry.at[k, 0], rx2.at[k], b_s.at[k, 2], bx_r.at[k, 1], xn[1])

    def b_y(k):
        return rcopy(rx.at[k, 0, rows((1 - yh) * 2 * q, 2 * q)], ry.at[k, 1], b_s.at[k, 4], by_r.at[k, 1], yhn)

    def b_g(k, d):
        return same(low.at[k, lrows(x, yh)], b_s.at[k, 4 + d], bg_r.at[k, d - 1], xn[d - 1])

    def b_g_in(k, d):
        return same(low.at[k, lrows(mod4(x - d), yh)], b_s.at[k, 4 + d], bg_r.at[k, d - 1], xn[d - 1])

    def b_h(k):
        return same(low.at[k, lrows(x, yh)], b_s.at[k, 8], bh_r.at[k, 0], yhn)

    def b_h_in(k):
        return same(low.at[k, lrows(x, 1 - yh)], b_s.at[k, 8], bh_r.at[k, 0], yhn)

    def b_gf(k, d):
        return same(low.at[k, lrows(x, 1 - yh)], b_s.at[k, 8 + d], bgf_r.at[k, d - 1], xn[d - 1])

    def b_gf_in(k, d):
        return same(low.at[k, lrows(mod4(x - d), 1 - yh)], b_s.at[k, 8 + d], bgf_r.at[k, d - 1], xn[d - 1])

    def b_hf(k):
        return same(low.at[k, lrows(x2, yh)], b_s.at[k, 10], bh_r.at[k, 1], yhn)

    def b_hf_in(k):
        return same(low.at[k, lrows(x2, 1 - yh)], b_s.at[k, 10], bh_r.at[k, 1], yhn)

    def part(k, l, zz):
        return p2.at[k % S2, rows(slot(c, l, zz), q)]

    def c_c(k):
        return rcopy(p2.at[k % S2, rows(slot(1 - c, 0, 0), 8 * q)], rc.at[k], c_s.at[k, 0], cc_r.at[k], cn)

    def c_y1(k):
        return rcopy(part(k, 1 - yl, z2), rl.at[k, 0], c_s.at[k, 1], cy_r.at[k, 0], yln)

    def c_zd(k, d):
        return rcopy(part(k, yl, mod4(z + d)), rz.at[k, d // 2, 0], c_s.at[k, 1 + d], cz_r.at[k, d // 2, 0], zn[d - 1])

    def c_zr(k, d):
        return rcopy(part(k, 1 - yl, mod4(z + d)), rz.at[k, d // 2, 1], c_s.at[k, 4 + d], cz_r.at[k, d // 2, 1], zn[d - 1])

    def c_z2(k):
        return rcopy(rl.at[k, 0], rz2.at[k], c_s.at[k, 3], cz2_r.at[k], zn[1])

    def c_y(k):
        return rcopy(rz.at[k, 0, 1], rl.at[k, 1], c_s.at[k, 6], cy_r.at[k, 1], yln)

    def A1(k):
        qg[k, mine] = qin[rows(k * q, q)]
        a_y(k).start()
        for d in (2, 1, 3):
            a_z(k, d).start()

    def A2y(k):
        a_y_in(k).wait_recv()
        for d in (1, 3):
            a_zf(k, d).start()

    def A2z(k):
        a_z_in(k, 2).wait_recv()
        a_yf(k).start()

    def A2c(k):
        for d in (1, 3):
            a_z_in(k, d).wait_recv()
        a_c(k, 0).start()

    def A3(k):
        a_yf_in(k).wait_recv()
        for d in (1, 3):
            a_zf_in(k, d).wait_recv()
        a_c(k, 1).start()

    def M1(k):
        a_c_in(k, 0).wait_recv()
        a_c_in(k, 1).wait_recv()
        if k >= S1:
            b_y1(k - S1).wait_send()
            for d in (1, 3):
                b_x(k - S1, d).wait_send()

        def split(i, _):
            part = rows(i * 16, 16)
            v = qg[k, part]
            hi = v.astype(BF16)
            qs[part] = hi
            qs[rows(16 * q + i * 16, 16)] = (v - hi.astype(F32)).astype(BF16)
            return 0

        lax.fori_loop(0, q, split, 0)
        for j in range(0, N1, T1):
            cols = pl.ds(j, T1)
            both = jnp.dot(qs[...], phi[:, cols], preferred_element_type=F32)
            third = jnp.dot(qs[: 16 * q], plo[:, cols], preferred_element_type=F32)
            p1[k % S1, :, cols] = both[: 16 * q] + (both[16 * q :] + third)
        b_y1(k).start()
        for d in (1, 3):
            b_x(k, d).start()

    def B1y(k):
        b_y1(k).wait_recv()
        ry[k, 0] = ry[k, 0] + p1[k % S1, lrows(x2, yh)]
        b_x2(k).start()

    def B2(k):
        for d in (1, 3):
            b_x(k, d).wait_recv()

        def total(h):
            there = rows(h * 2 * q, 2 * q)
            return p1[k % S1, lrows(x, h)] + (rx[k, 0, there] + rx[k, 1, there])

        rx[k, 0, rows((1 - yh) * 2 * q, 2 * q)] = total(1 - yh)
        b_y(k).start()
        low[k, lrows(x, yh)] = total(yh)

    def B3(k):
        b_y(k).wait_recv()
        b_x2(k).wait_recv()
        here = lrows(x, yh)
        v = ((low[k, here] + ry[k, 1]) + rx2[k]) * gain[...]
        low[k, here] = v.astype(BF16).astype(F32)
        b_h(k).start()
        for d in (2, 1, 3):
            b_g(k, d).start()

    def B5(k):
        b_h_in(k).wait_recv()
        for d in (1, 3):
            b_gf(k, d).start()

    def B6a(k):
        b_g_in(k, 2).wait_recv()
        b_hf(k).start()

    def M2(k):
        for d in (1, 3):
            b_g_in(k, d).wait_recv()
            b_gf_in(k, d).wait_recv()
        b_hf_in(k).wait_recv()
        if k >= S2:
            c_c(k - S2).wait_send()
            c_y1(k - S2).wait_send()
            for d in (1, 3):
                c_zd(k - S2, d).wait_send()
                c_zr(k - S2, d).wait_send()
        lowb[...] = low[k].astype(BF16)

        def tile(j, _):
            cols = pl.ds(pl.multiple_of(j * T2, T2), T2)
            p2[k % S2, :, cols] = jnp.dot(lowb[...], sv[:, cols], preferred_element_type=F32)
            return 0

        lax.fori_loop(0, N2 // T2, tile, 0)
        c_c(k).start()

    def C1(k):
        c_c(k).wait_recv()
        here = rows(slot(c, 0, 0), 8 * q)
        p2[k % S2, here] = p2[k % S2, here] + rc[k]
        c_y1(k).start()
        for d in (1, 3):
            c_zr(k, d).start()
        for d in (1, 3):
            c_zd(k, d).start()

    def C1y(k):
        c_y1(k).wait_recv()
        rl[k, 0] = rl[k, 0] + part(k, yl, z2)[...]
        c_z2(k).start()

    def C2(k):
        for d in (1, 3):
            c_zr(k, d).wait_recv()
        rz[k, 0, 1] = part(k, 1 - yl, z)[...] + (rz[k, 0, 1] + rz[k, 1, 1])
        c_y(k).start()

    def C3(k):
        for d in (1, 3):
            c_zd(k, d).wait_recv()
        c_y(k).wait_recv()
        c_z2(k).wait_recv()
        out[rows(k * q, q)] = (part(k, yl, z)[...] + (rz[k, 0, 0] + rz[k, 1, 0])) + (rl[k, 1] + rz2[k])

    barrier = pltpu.get_barrier_semaphore()
    for peer in xn + zn + [yln, yhn, cn]:
        pl.semaphore_signal(barrier, inc=1, device_id=peer, device_id_type=MESH)

    def p_in(i):
        there = pl.ds(pl.multiple_of(i * PT, PT), PT)
        return pltpu.make_async_copy(precond.at[there], stage.at[lax.rem(i, NB)], pt_sem.at[lax.rem(i, NB)])

    def s_in(i):
        there = pl.ds(pl.multiple_of(i * 256, 256), 256)
        return pltpu.make_async_copy(store.at[there], sst.at[lax.rem(i, 2)], st_sem.at[lax.rem(i, 2)])

    for i in range(NB):
        p_in(i).start()
    s_in(0).start()
    s_in(1).start()

    def split_p(i, _):
        p_in(i).wait()
        part = pl.ds(pl.multiple_of(i * PT, PT), PT)
        v = stage[lax.rem(i, NB)]
        hi = v.astype(BF16)
        phi[part] = hi
        plo[part] = (v - hi.astype(F32)).astype(BF16)

        @pl.when(i + NB < K // PT)
        def _():
            p_in(i + NB).start()

        return 0

    def turn(i, _):
        s_in(i).wait()
        sv[:, pl.ds(pl.multiple_of(i * 256, 256), 256)] = sst[lax.rem(i, 2)].T

        @pl.when(i + 2 < N2 // 256)
        def _():
            s_in(i + 2).start()

        return 0

    def PR(i):
        lax.fori_loop(i * (K // PT) // 2, (i + 1) * (K // PT) // 2, split_p, 0)

    def ST(i):
        lax.fori_loop(i * (N2 // 256) // 3, (i + 1) * (N2 // 256) // 3, turn, 0)

    pl.semaphore_wait(barrier, 9)
    steps = dict(
        PR=PR, ST=ST, A1=A1, A2y=A2y, A2z=A2z, A2c=A2c, A3=A3, M1=M1, B1y=B1y, B2=B2, B3=B3, B5=B5, B6a=B6a,
        M2=M2, C1=C1, C1y=C1y, C2=C2, C3=C3,
    )
    for name, k in ORDER:
        steps[name](k)

    for k in range(n):
        for d in (1, 2, 3):
            a_z(k, d).wait_send()
            b_g(k, d).wait_send()
        a_y(k).wait_send()
        a_yf(k).wait_send()
        for d in (1, 3):
            a_zf(k, d).wait_send()
            b_gf(k, d).wait_send()
        a_c(k, 0).wait_send()
        a_c(k, 1).wait_send()
        b_x2(k).wait_send()
        b_y(k).wait_send()
        b_h(k).wait_send()
        b_hf(k).wait_send()
        c_z2(k).wait_send()
        c_y(k).wait_send()
        if k >= n - S1:
            b_y1(k).wait_send()
            for d in (1, 3):
                b_x(k, d).wait_send()
        if k >= n - S2:
            c_c(k).wait_send()
            c_y1(k).wait_send()
            for d in (1, 3):
                c_zd(k, d).wait_send()
                c_zr(k, d).wait_send()


def local(queries, precond, column_gain, store):
    b, own, K = queries.shape
    q, N1, N2 = Q, precond.shape[1], store.shape[0]
    n = b * own // q
    vm = pltpu.VMEM
    dma = pltpu.SemaphoreType.DMA
    out = pl.pallas_call(
        functools.partial(kernel, n),
        out_shape=jax.ShapeDtypeStruct((b * own, N2), F32),
        in_specs=[
            pl.BlockSpec(memory_space=pltpu.VMEM),
            pl.BlockSpec(memory_space=pltpu.VMEM),
            pl.BlockSpec(memory_space=pl.ANY),
            pl.BlockSpec(memory_space=pl.ANY),
        ],
        out_specs=pl.BlockSpec(memory_space=pltpu.VMEM),
        scratch_shapes=[
            vm((n, 16 * q, K), F32),
            vm((32 * q, K), BF16),
            vm((K, N1), BF16),
            vm((K, N1), BF16),
            vm((NB, PT, N1), F32),
            vm((S1, 16 * q, N1), F32),
            vm((n, 2, 4 * q, N1), F32),
            vm((n, 2 * q, N1), F32),
            vm((n, 2, 2 * q, N1), F32),
            vm((n, 16 * q, N1), F32),
            vm((16 * q, N1), BF16),
            vm((N1, N2), BF16),
            vm((2, 256, N1), BF16),
            vm((S2, 16 * q, N2), F32),
            vm((n, 8 * q, N2), F32),
            vm((n, 2, 2, q, N2), F32),
            vm((n, q, N2), F32),
            vm((n, 2, q, N2), F32),
            dma((NB,)),
            dma((2,)),
            dma((n, 9)),
            dma((n, 3)),
            dma((n, 3)),
            dma((n, 2)),
            dma((n, 2)),
            dma((n, 12)),
            dma((n, 3)),
            dma((n, 2)),
            dma((n, 2)),
            dma((n, 3)),
            dma((n, 3)),
            dma((n, 8)),
            dma((n,)),
            dma((n, 2, 2)),
            dma((n,)),
            dma((n, 2)),
        ],
        compiler_params=pltpu.CompilerParams(
            collective_id=0, has_side_effects=True, vmem_limit_bytes=63 * 1024 * 1024
        ),
        cost_estimate=pl.CostEstimate(flops=2 * 16 * b * own * (3 * K * N1 + N1 * N2), bytes_accessed=24 << 20, transcendentals=0),
        name="scores",
    )(queries.reshape(b * own, K), column_gain.reshape(1, N1), precond, store)
    return out.reshape(b, own, N2)


def solution(mesh):
    return jax.shard_map(
        local,
        mesh=mesh,
        in_specs=(P(None, "col", "row"), P("row", "col"), P("col"), P("row", "col")),
        out_specs=P(None, "col", "row"),
        check_vma=False,
    )
```

time: 187 us -> 132 us (0.71)
  Pallas kernels: 183 us -> 128 us
    pallas_call x1, Pallas kernels: 183 us -> 128 us  [local(): pl.pallas_call(functools.partial(kernel, n), out_shape=jax.ShapeDtypeStru...]
where the time goes in v2:
time: 132 us; the launch traced here: 131 us
  Pallas kernels  128 us (97%)
  local copies, waits for them, and re-layouts  3.21 us (2%)
    pallas_call x1, Pallas kernels, local(): pl.pallas_call(functools.partial(kernel, n), out_shape=jax.ShapeDtypeStru...  128 us

profile of v2, /device:TPU:1, one launch (start us, length us, event | category | flops | bytes accessed | tf_op | source)
XLA Modules:
  0.0 131.2 jit_solution(2946015769621314292)
XLA Ops:
  0.0 1.3 reshape.10.gain
  1.3 128.0 %scores.1 = f32[48,3072]{1,0:T(8,128)} custom-call(f32[48,2560]{1,0:T(8,128)} %bitcast.3, f32[1,1280]{1,0:T(1,128)} %reshape.10.gain, f32[2560,1280]{1,0:T(8,128)} %precond.1, bf16[3072,1280]{1,0:T(8,128)(2,1)} %store.1), custom_call_target="tpu_custom_call" | custom-call | flops 21139292160 | bytes 25165824 | tf_op jit(solution)/shard_map/scores/pallas_call | solution.py:396
  129.3 1.9 %copy.6 = f32[2,24,3072]{2,1,0:T(8,128)} copy(f32[2,24,3072]{2,1,0:T(8,128)} %bitcast.2) | data formatting | bytes 1179648

commit v3 on v2

--- a/solution.py
+++ b/solution.py
@@ -10,21 +10,22 @@
 MESH = pl.DeviceIdType.MESH
 Q = 8
 PT, NB = 128, 4
+NS = 4
 S1, S2 = 3, 3
 T1, T2 = 1280, 1024
 ORDER = (
-    ("A1", 0), ("A1", 1), ("PR", 0), ("PR", 1), ("A2y", 0), ("A2y", 1), ("A2z", 0), ("A2c", 0), ("ST", 0),
-    ("A2z", 1), ("A2c", 1), ("ST", 1), ("ST", 2), ("A3", 0), ("A1", 2), ("A3", 1), ("A1", 3), ("M1", 0),
-    ("A2y", 2), ("A2y", 3), ("M1", 1), ("B1y", 0), ("A2z", 2), ("A2c", 2), ("A2z", 3), ("A2c", 3), ("B2", 0),
-    ("B1y", 1), ("B2", 1), ("A3", 2), ("A3", 3), ("A1", 4), ("B3", 0), ("A1", 5), ("B3", 1), ("M1", 2),
-    ("M1", 3), ("B5", 0), ("B6a", 0), ("A2y", 4), ("B5", 1), ("B6a", 1), ("A2z", 4), ("A2c", 4), ("A2y", 5),
-    ("A2z", 5), ("A2c", 5), ("B1y", 2), ("B1y", 3), ("M2", 0), ("B2", 2), ("A3", 4), ("A3", 5), ("M2", 1),
-    ("B2", 3), ("B3", 2), ("M1", 4), ("C1", 0), ("C1", 1), ("B5", 2), ("B3", 3), ("B6a", 2), ("M1", 5),
-    ("B1y", 4), ("B6a", 3), ("C1y", 0), ("C2", 0), ("B5", 3), ("M2", 2), ("C1y", 1), ("C2", 1), ("B2", 4),
-    ("B1y", 5), ("C1", 2), ("C3", 0), ("B2", 5), ("M2", 3), ("B3", 4), ("C3", 1), ("C1", 3), ("B3", 5),
-    ("C1y", 2), ("C2", 2), ("B6a", 4), ("B5", 4), ("B6a", 5), ("C1y", 3), ("C2", 3), ("B5", 5), ("M2", 4),
-    ("C3", 2), ("M2", 5), ("C3", 3), ("C1", 4), ("C1", 5), ("C1y", 4), ("C1y", 5), ("C2", 4), ("C3", 4),
-    ("C2", 5), ("C3", 5),
+    ("A1", 0), ("PR", 0), ("A2y", 0), ("A1", 1), ("A2z", 0), ("PR", 1), ("A2c", 0), ("A2y", 1), ("A1", 2),
+    ("A3", 0), ("A2z", 1), ("A2c", 1), ("M1", 0), ("A3", 1), ("A2y", 2), ("A1", 3), ("A2z", 2), ("M1", 1),
+    ("B1y", 0), ("A2y", 3), ("A2c", 2), ("A3", 2), ("A1", 4), ("A2z", 3), ("B2", 0), ("B1y", 1), ("M1", 2),
+    ("B2", 1), ("A2c", 3), ("A2y", 4), ("A3", 3), ("ST", 0), ("A2z", 4), ("B3", 0), ("M1", 3), ("ST", 1),
+    ("A1", 5), ("ST", 2), ("A2c", 4), ("A3", 4), ("B1y", 2), ("B5", 0), ("B2", 2), ("B6a", 0), ("A2z", 5),
+    ("B3", 1), ("A2y", 5), ("A2c", 5), ("B3", 2), ("M1", 4), ("B5", 1), ("B1y", 3), ("B6a", 1), ("A3", 5),
+    ("M2", 0), ("B2", 3), ("B5", 2), ("C1", 0), ("B6a", 2), ("M1", 5), ("B3", 3), ("C1y", 0), ("C2", 0),
+    ("B1y", 4), ("M2", 2), ("B2", 4), ("B5", 3), ("B1y", 5), ("C1", 2), ("B6a", 3), ("M2", 1), ("B3", 4),
+    ("B2", 5), ("C1y", 2), ("C1", 1), ("M2", 3), ("B6a", 4), ("B5", 4), ("C1y", 1), ("C1", 3), ("B3", 5),
+    ("C2", 1), ("M2", 4), ("B6a", 5), ("C1y", 3), ("B5", 5), ("C1", 4), ("C3", 1), ("C3", 0), ("C2", 2),
+    ("M2", 5), ("C2", 3), ("C1y", 4), ("C2", 4), ("C3", 2), ("C1", 5), ("C1y", 5), ("C3", 4), ("C2", 5),
+    ("C3", 3), ("C3", 5),
 )
 F32, BF16 = jnp.float32, jnp.bfloat16
 
@@ -239,7 +240,7 @@
         b_y(k).wait_recv()
         b_x2(k).wait_recv()
         here = lrows(x, yh)
-        v = ((low[k, here] + ry[k, 1]) + rx2[k]) * gain[...]
+        v = ((low[k, here] + ry[k, 1]) + rx2[k]) * gain[...].reshape(1, -1)
         low[k, here] = v.astype(BF16).astype(F32)
         b_h(k).start()
         for d in (2, 1, 3):
@@ -295,13 +296,15 @@
             c_zr(k, d).wait_recv()
         rz[k, 0, 1] = part(k, 1 - yl, z)[...] + (rz[k, 0, 1] + rz[k, 1, 1])
         c_y(k).start()
+        out[rows(k * q, q)] = part(k, yl, z)[...]
 
     def C3(k):
         for d in (1, 3):
             c_zd(k, d).wait_recv()
         c_y(k).wait_recv()
         c_z2(k).wait_recv()
-        out[rows(k * q, q)] = (part(k, yl, z)[...] + (rz[k, 0, 0] + rz[k, 1, 0])) + (rl[k, 1] + rz2[k])
+        here = rows(k * q, q)
+        out[here] = (out[here] + (rz[k, 0, 0] + rz[k, 1, 0])) + (rl[k, 1] + rz2[k])
 
     barrier = pltpu.get_barrier_semaphore()
     for peer in xn + zn + [yln, yhn, cn]:
@@ -313,12 +316,12 @@
 
     def s_in(i):
         there = pl.ds(pl.multiple_of(i * 256, 256), 256)
-        return pltpu.make_async_copy(store.at[there], sst.at[lax.rem(i, 2)], st_sem.at[lax.rem(i, 2)])
+        return pltpu.make_async_copy(store.at[there], sst.at[lax.rem(i, NS)], st_sem.at[lax.rem(i, NS)])
 
     for i in range(NB):
         p_in(i).start()
-    s_in(0).start()
-    s_in(1).start()
+    for i in range(NS):
+        s_in(i).start()
 
     def split_p(i, _):
         p_in(i).wait()
@@ -336,11 +339,11 @@
 
     def turn(i, _):
         s_in(i).wait()
-        sv[:, pl.ds(pl.multiple_of(i * 256, 256), 256)] = sst[lax.rem(i, 2)].T
-
-        @pl.when(i + 2 < N2 // 256)
+        sv[:, pl.ds(pl.multiple_of(i * 256, 256), 256)] = sst[lax.rem(i, NS)].T
+
+        @pl.when(i + NS < N2 // 256)
         def _():
-            s_in(i + 2).start()
+            s_in(i + NS).start()
 
         return 0
 
@@ -416,14 +419,14 @@
             vm((n, 16 * q, N1), F32),
             vm((16 * q, N1), BF16),
             vm((N1, N2), BF16),
-            vm((2, 256, N1), BF16),
+            vm((NS, 256, N1), BF16),
             vm((S2, 16 * q, N2), F32),
             vm((n, 8 * q, N2), F32),
             vm((n, 2, 2, q, N2), F32),
             vm((n, q, N2), F32),
             vm((n, 2, q, N2), F32),
             dma((NB,)),
-            dma((2,)),
+            dma((NS,)),
             dma((n, 9)),
             dma((n, 3)),
             dma((n, 3)),
@@ -446,7 +449,7 @@
         ),
         cost_estimate=pl.CostEstimate(flops=2 * 16 * b * own * (3 * K * N1 + N1 * N2), bytes_accessed=24 << 20, transcendentals=0),
         name="scores",
-    )(queries.reshape(b * own, K), column_gain.reshape(1, N1), precond, store)
+    )(queries.reshape(b * own, K), column_gain, precond, store)
     return out.reshape(b, own, N2)
 
 

time: 132 us -> 115 us (0.87)
  Pallas kernels: 128 us -> 113 us
    pallas_call x1, Pallas kernels: 128 us -> 113 us  [local(): pl.pallas_call(functools.partial(kernel, n), out_shape=jax.ShapeDtypeStru...]
where the time goes in v3:
time: 115 us; the launch traced here: 114 us
  Pallas kernels  113 us (98%)
  local copies, waits for them, and re-layouts  1.92 us (2%)
    pallas_call x1, Pallas kernels, local(): pl.pallas_call(functools.partial(kernel, n), out_shape=jax.ShapeDtypeStru...  113 us

profile of v3, /device:TPU:1, one launch (start us, length us, event | category | flops | bytes accessed | tf_op | source)
XLA Modules:
  0.0 114.5 jit_solution(10961619329944718488)
XLA Ops:
  0.0 112.6 %scores.1 = f32[48,3072]{1,0:T(8,128)} custom-call(f32[48,2560]{1,0:T(8,128)} %bitcast.3, f32[1280]{0:T(1024)} %gain.1, f32[2560,1280]{1,0:T(8,128)} %precond.1, bf16[3072,1280]{1,0:T(8,128)(2,1)} %store.1), custom_call_target="tpu_custom_call" | custom-call | flops 21139292160 | bytes 25165824 | tf_op jit(solution)/shard_map/scores/pallas_call | solution.py:399
  112.6 1.9 %copy.6 = f32[2,24,3072]{2,1,0:T(8,128)} copy(f32[2,24,3072]{2,1,0:T(8,128)} %bitcast.2) | data formatting | bytes 1179648

commit v4 on v3

v4 whole, which is shorter than its diff:
```python
import functools

import jax
import jax.numpy as jnp
from jax import lax
from jax.experimental import pallas as pl
from jax.experimental.pallas import tpu as pltpu
from jax.sharding import PartitionSpec as P

MESH = pl.DeviceIdType.MESH
Q = 8
PT, NB = 128, 4
NS = 4
S1, S2 = 3, 3
CUT = 768
BS, CS = 2, 2
ORDER = (
    ("A1", 0), ("PR", 0), ("A2y", 0), ("A1", 1), ("A2z", 0), ("PR", 1), ("A2y", 1), ("A2c", 0), ("A1", 2),
    ("A3", 0), ("A2z", 1), ("A2c", 1), ("M1", 0), ("A2y", 2), ("A1", 3), ("A3", 1), ("M1", 1), ("A2z", 2),
    ("M1", 2), ("A2c", 2), ("M1", 3), ("B1y", 1), ("B2", 1), ("A3", 2), ("B1y", 0), ("A2z", 3), ("A1", 4),
    ("B2", 0), ("A2y", 3), ("B1y", 2), ("M1", 4), ("M1", 5), ("B3", 0), ("B2", 2), ("ST", 0), ("A2z", 4),
    ("B1y", 3), ("A2c", 3), ("A1", 5), ("B2", 3), ("A3", 3), ("B1y", 4), ("B1y", 5), ("B3", 1), ("M1", 6),
    ("A2y", 4), ("M1", 7), ("B3", 2), ("B5", 1), ("B2", 4), ("B3", 3), ("B2", 5), ("A2z", 5), ("B6a", 0),
    ("B6a", 1), ("B5", 0), ("A2c", 4), ("A2y", 5), ("A3", 4), ("B1y", 6), ("ST", 1), ("A2c", 5), ("ST", 2),
    ("M1", 8), ("B2", 6), ("B1y", 7), ("B6a", 2), ("M1", 9), ("B5", 3), ("B5", 2), ("A3", 5), ("B6a", 3),
    ("B2", 7), ("B3", 4), ("M2", 0), ("M2", 1), ("B3", 6), ("C1", 0), ("C1", 1), ("B3", 5), ("M1", 10),
    ("B6a", 4), ("C1y", 0), ("B5", 4), ("B1y", 8), ("B3", 7), ("B1y", 9), ("B2", 8), ("M2", 2), ("C1y", 1),
    ("B6a", 6), ("B5", 5), ("B2", 9), ("C1", 2), ("B6a", 5), ("M2", 3), ("C2", 1), ("M1", 11), ("B5", 7),
    ("C2", 0), ("C1y", 2), ("C1", 3), ("B3", 8), ("M2", 4), ("B6a", 7), ("B5", 6), ("M2", 5), ("B1y", 10),
    ("B2", 10), ("C1", 4), ("C1", 5), ("B3", 9), ("B5", 8), ("B6a", 8), ("B1y", 11), ("B2", 11), ("M2", 6),
    ("C3", 0), ("C1y", 4), ("B3", 10), ("C1y", 3), ("M2", 7), ("C1", 6), ("C1y", 5), ("B5", 9), ("B6a", 9),
    ("C1", 7), ("B3", 11), ("C1y", 6), ("C2", 3), ("C2", 2), ("B6a", 10), ("B5", 10), ("M2", 8), ("M2", 9),
    ("B6a", 11), ("C1y", 7), ("B5", 11), ("C1", 8), ("C1", 9), ("C3", 2), ("C2", 6), ("C2", 4), ("C2", 5),
    ("C3", 3), ("M2", 10), ("C3", 1), ("C2", 7), ("C1y", 8), ("M2", 11), ("C1", 10), ("C3", 6), ("C1", 11),
    ("C3", 4), ("C2", 8), ("C1y", 10), ("C1y", 9), ("C2", 10), ("C2", 9), ("C1y", 11), ("C3", 8), ("C2", 11),
    ("C3", 10), ("C3", 7), ("C3", 9), ("C3", 5), ("C3", 11),
)
F32, BF16 = jnp.float32, jnp.bfloat16


def kernel(
    n, qin, gain, precond, store, result,
    qg, qs, phi, plo, stage, p1, rx, rx2, ry, low, lowb, sv, sst, p2, rc, rz, rz2, rl, out,
    q_sem, o_sem, pt_sem, st_sem, a_s, az_r, ay_r, ac_r, b_s, bx_r, by_r, bh_r, bg_r, c_s, cc_r, cz_r, cy_r,
):
    q = Q
    K, N1, N2 = phi.shape[0], phi.shape[1], sv.shape[1]
    row, col = lax.axis_index("row"), lax.axis_index("col")
    x, yh = row // 2, lax.rem(row, 2)
    yl, z, c = col // 8, lax.rem(col // 2, 4), lax.rem(col, 2)

    def dev(x=x, yh=yh, yl=yl, z=z, c=c):
        return (x * 2 + yh, yl * 8 + z * 2 + c)

    def mod4(v):
        return lax.rem(v + 4, 4)

    xn = [dev(x=mod4(x + d)) for d in (1, 2, 3)]
    zn = [dev(z=mod4(z + d)) for d in (1, 2, 3)]
    yln, yhn, cn = dev(yl=1 - yl), dev(yh=1 - yh), dev(c=1 - c)

    def rows(start, size):
        return pl.ds(pl.multiple_of(start, q), size)

    def slot(c, yl, z):
        return ((c * 2 + yl) * 4 + z) * q

    mine = rows(slot(c, yl, z), q)

    def rcopy(src, dst, ssem, rsem, device):
        return pltpu.make_async_remote_copy(
            src_ref=src, dst_ref=dst, send_sem=ssem, recv_sem=rsem, device_id=device, device_id_type=MESH
        )

    def at_slot(k, c, l, zz, count=1):
        return qg.at[k, rows(slot(c, l, zz), count * q)]

    def same(there, ssem, rsem, device):
        return rcopy(there, there, ssem, rsem, device)

    def own(k):
        return qg.at[k, mine]

    def q_in(k):
        return pltpu.make_async_copy(qin.at[rows(k * q, q)], qg.at[k, mine], q_sem.at[k])

    def a_z(k, d):
        return rcopy(own(k), qg.at[k, mine], a_s.at[k], az_r.at[k, d % 2], zn[d - 1])

    def a_y(k):
        return rcopy(own(k), qg.at[k, mine], a_s.at[k], ay_r.at[k, 0], yln)

    def a_zf(k, d):
        return same(at_slot(k, c, 1 - yl, z), a_s.at[k], ay_r.at[k, 1], zn[d - 1])

    def a_yf(k):
        return same(at_slot(k, c, yl, mod4(z + 2)), a_s.at[k], ay_r.at[k, 1], yln)

    def a_c(k, i):
        return same(at_slot(k, c, yl if i == 0 else 1 - yl, 0, 4), a_s.at[k], ac_r.at[k], cn)

    def lrows(x, yh):
        return rows(x * 4 * q + yh * 2 * q, 2 * q)

    x2 = mod4(x + 2)
    z2 = mod4(z + 2)

    def b_y1(k):
        return rcopy(p1.at[k % (S1 * BS), lrows(x2, 1 - yh)], ry.at[k, 0], b_s.at[k, 0], by_r.at[k], yhn)

    def b_x(k, d):
        src = p1.at[k % (S1 * BS), rows(mod4(x + d) * 4 * q, 4 * q)]
        return rcopy(src, rx.at[k, d // 2], b_s.at[k, 0], bx_r.at[k, 0], xn[d - 1])

    def b_x2(k):
        return rcopy(ry.at[k, 0], rx2.at[k], b_s.at[k, 1], bx_r.at[k, 1], xn[1])

    def b_y(k):
        return rcopy(rx.at[k, 0, rows((1 - yh) * 2 * q, 2 * q)], ry.at[k, 1], b_s.at[k, 1], bx_r.at[k, 1], yhn)

    def b_g(k, d):
        return same(low.at[k, lrows(x, yh)], b_s.at[k, 2], (bh_r.at[k, 1] if d == 2 else bg_r.at[k]), xn[d - 1])

    def b_h(k):
        return same(low.at[k, lrows(x, yh)], b_s.at[k, 2], bh_r.at[k, 0], yhn)

    def b_gf(k, d):
        return same(low.at[k, lrows(x, 1 - yh)], b_s.at[k, 2], bg_r.at[k], xn[d - 1])

    def b_hf(k):
        return same(low.at[k, lrows(x2, yh)], b_s.at[k, 2], bg_r.at[k], yhn)

    def part(k, l, zz):
        return p2.at[k % (S2 * CS), rows(slot(c, l, zz), q)]

    def c_c(k):
        return rcopy(p2.at[k % (S2 * CS), rows(slot(1 - c, 0, 0), 8 * q)], rc.at[k], c_s.at[k, 0], cc_r.at[k], cn)

    def c_y1(k):
        return rcopy(part(k, 1 - yl, z2), rl.at[k, 0], c_s.at[k, 0], cy_r.at[k], yln)

    def c_zd(k, d):
        return rcopy(part(k, yl, mod4(z + d)), rz.at[k, d // 2, 0], c_s.at[k, 0], cz_r.at[k, 1], zn[d - 1])

    def c_zr(k, d):
        return rcopy(part(k, 1 - yl, mod4(z + d)), rz.at[k, d // 2, 1], c_s.at[k, 0], cz_r.at[k, 0], zn[d - 1])

    def c_z2(k):
        return rcopy(rl.at[k, 0], rz2.at[k], c_s.at[k, 1], cz_r.at[k, 1], zn[1])

    def c_y(k):
        return rcopy(rz.at[k, 0, 1], rl.at[k, 1], c_s.at[k, 1], cz_r.at[k, 1], yln)

    def came(like, sem):
        rcopy(like, like, sem, sem, cn).wait_recv()

    def went(like, sem):
        rcopy(like, like, sem, sem, cn).wait_send()

    def A1(k):
        q_in(k).wait()
        a_y(k).start()
        for d in (2, 1, 3):
            a_z(k, d).start()

    def A2y(k):
        came(qg.at[k, pl.ds(0, q)], ay_r.at[k, 0])
        for d in (1, 3):
            a_zf(k, d).start()

    def A2z(k):
        came(qg.at[k, pl.ds(0, q)], az_r.at[k, 0])
        a_yf(k).start()

    def A2c(k):
        came(qg.at[k, pl.ds(0, 2 * q)], az_r.at[k, 1])
        a_c(k, 0).start()

    def A3(k):
        came(qg.at[k, pl.ds(0, 3 * q)], ay_r.at[k, 1])
        a_c(k, 1).start()

    def M1(k):
        b, h = k // BS, k % BS
        if h == 0:
            came(qg.at[b, pl.ds(0, 8 * q)], ac_r.at[b])
            if b >= S1:
                for old in range(k - S1 * BS, k - S1 * BS + BS):
                    went(p1.at[old % (S1 * BS), pl.ds(0, 10 * q)], b_s.at[old, 0])

            def split(i, _):
                part = rows(i * 16, 16)
                v = qg[b, part]
                hi = v.astype(BF16)
                qs[part] = hi
                qs[rows(16 * q + i * 16, 16)] = (v - hi.astype(F32)).astype(BF16)
                return 0

            lax.fori_loop(0, q, split, 0)
        half = N1 // BS
        first, last = (0, CUT) if h == 0 else (CUT, N1)
        cols = pl.ds(first, last - first)
        both = jnp.dot(qs[...], phi[:, cols], preferred_element_type=F32)
        third = jnp.dot(qs[: 16 * q], plo[:, cols], preferred_element_type=F32)
        product = both[: 16 * q] + (both[16 * q :] + third)
        if h == 0:
            p1[k % (S1 * BS)] = product[:, :half]
            p1[(k + 1) % (S1 * BS), :, : CUT - half] = product[:, half:]
        else:
            p1[k % (S1 * BS), :, CUT - half :] = product
        b_y1(k).start()
        for d in (1, 3):
            b_x(k, d).start()

    def B1y(k):
        came(ry.at[k, 0], by_r.at[k])
        ry[k, 0] = ry[k, 0] + p1[k % (S1 * BS), lrows(x2, yh)]
        b_x2(k).start()

    def B2(k):
        came(rx.at[k], bx_r.at[k, 0])

        def total(h):
            there = rows(h * 2 * q, 2 * q)
            return p1[k % (S1 * BS), lrows(x, h)] + (rx[k, 0, there] + rx[k, 1, there])

        rx[k, 0, rows((1 - yh) * 2 * q, 2 * q)] = total(1 - yh)
        b_y(k).start()
        low[k, lrows(x, yh)] = total(yh)

    def gain_part(h):
        return gain[pl.ds(h * (N1 // BS), N1 // BS)].reshape(1, -1)

    def B3(k):
        came(ry.at[k], bx_r.at[k, 1])
        here = lrows(x, yh)
        v = ((low[k, here] + ry[k, 1]) + rx2[k]) * gain_part(k % BS)
        low[k, here] = v.astype(BF16).astype(F32)
        b_h(k).start()
        for d in (2, 1, 3):
            b_g(k, d).start()

    def B5(k):
        came(rx2.at[k], bh_r.at[k, 0])
        for d in (1, 3):
            b_gf(k, d).start()

    def B6a(k):
        came(rx2.at[k], bh_r.at[k, 1])
        b_hf(k).start()

    def M2(k):
        b, h = k // CS, k % CS
        if h == 0:
            for part in range(b * BS, b * BS + BS):
                came(low.at[part, pl.ds(0, 10 * q)], bg_r.at[part])
                h0 = part % BS * (N1 // BS)
                lowb[:, h0 : h0 + N1 // BS] = low[part].astype(BF16)
                went(ry.at[part], b_s.at[part, 1])
            went(qg.at[b, pl.ds(0, 15 * q)], a_s.at[b])
            if b >= S2:
                for old in range(k - S2 * CS, k - S2 * CS + CS):
                    went(p2.at[old % (S2 * CS), pl.ds(0, 13 * q)], c_s.at[old, 0])
        cols = pl.ds(h * (N2 // CS), N2 // CS)
        p2[k % (S2 * CS)] = jnp.dot(lowb[...], sv[:, cols], preferred_element_type=F32)
        c_c(k).start()

    def C1(k):
        came(rc.at[k], cc_r.at[k])
        here = rows(slot(c, 0, 0), 8 * q)
        p2[k % (S2 * CS), here] = p2[k % (S2 * CS), here] + rc[k]
        c_y1(k).start()
        for d in (1, 3):
            c_zr(k, d).start()
        for d in (1, 3):
            c_zd(k, d).start()

    def C1y(k):
        came(rz2.at[k], cy_r.at[k])
        rl[k, 0] = rl[k, 0] + part(k, yl, z2)[...]
        c_z2(k).start()

    def C2(k):
        came(rl.at[k], cz_r.at[k, 0])
        rz[k, 0, 1] = part(k, 1 - yl, z)[...] + (rz[k, 0, 1] + rz[k, 1, 1])
        c_y(k).start()
        out[rows(k // CS * q, q), pl.ds(k % CS * (N2 // CS), N2 // CS)] = part(k, yl, z)[...]

    def C3(k):
        came(rz.at[k], cz_r.at[k, 1])
        here = rows(k // CS * q, q), pl.ds(k % CS * (N2 // CS), N2 // CS)
        out[here] = (out[here] + (rz[k, 0, 0] + rz[k, 1, 0])) + (rl[k, 1] + rz2[k])

    barrier = pltpu.get_barrier_semaphore()
    for peer in xn + zn + [yln, yhn, cn]:
        pl.semaphore_signal(barrier, inc=1, device_id=peer, device_id_type=MESH)

    def p_in(i):
        there = pl.ds(pl.multiple_of(i * PT, PT), PT)
        return pltpu.make_async_copy(precond.at[there], stage.at[lax.rem(i, NB)], pt_sem.at[lax.rem(i, NB)])

    def s_in(i):
        there = pl.ds(pl.multiple_of(i * 256, 256), 256)
        return pltpu.make_async_copy(store.at[there], sst.at[lax.rem(i, NS)], st_sem.at[lax.rem(i, NS)])

    for k in range(n):
        q_in(k).start()
    for i in range(NB):
        p_in(i).start()
    for i in range(NS):
        s_in(i).start()

    def split_p(i, _):
        p_in(i).wait()
        part = pl.ds(pl.multiple_of(i * PT, PT), PT)
        v = stage[lax.rem(i, NB)]
        hi = v.astype(BF16)
        phi[part] = hi
        plo[part] = (v - hi.astype(F32)).astype(BF16)

        @pl.when(i + NB < K // PT)
        def _():
            p_in(i + NB).start()

        return 0

    def turn(i, _):
        s_in(i).wait()
        sv[:, pl.ds(pl.multiple_of(i * 256, 256), 256)] = sst[lax.rem(i, NS)].T

        @pl.when(i + NS < N2 // 256)
        def _():
            s_in(i + NS).start()

        return 0

    def PR(i):
        lax.fori_loop(i * (K // PT) // 2, (i + 1) * (K // PT) // 2, split_p, 0)

    def ST(i):
        lax.fori_loop(i * (N2 // 256) // 3, (i + 1) * (N2 // 256) // 3, turn, 0)

    pl.semaphore_wait(barrier, 9)
    steps = dict(
        PR=PR, ST=ST, A1=A1, A2y=A2y, A2z=A2z, A2c=A2c, A3=A3, M1=M1, B1y=B1y, B2=B2, B3=B3, B5=B5, B6a=B6a,
        M2=M2, C1=C1, C1y=C1y, C2=C2, C3=C3,
    )
    def o_out(k):
        return pltpu.make_async_copy(out.at[rows(k * q, q)], result.at[rows(k * q, q)], o_sem.at[k])

    left = [CS] * n
    for name, k in ORDER:
        steps[name](k)
        if name == "C3":
            left[k // CS] -= 1
            if left[k // CS] == 0:
                o_out(k // CS).start()

    for k in range(n * BS):
        went(low.at[k, pl.ds(0, 14 * q)], b_s.at[k, 2])
        if k >= (n - S1) * BS:
            went(p1.at[k % (S1 * BS), pl.ds(0, 10 * q)], b_s.at[k, 0])
    for k in range(n):
        o_out(k).wait()
    for k in range(n * CS):
        went(rl.at[k], c_s.at[k, 1])
        if k >= (n - S2) * CS:
            went(p2.at[k % (S2 * CS), pl.ds(0, 13 * q)], c_s.at[k, 0])


def local(queries, precond, column_gain, store):
    b, own, K = queries.shape
    q, N1, N2 = Q, precond.shape[1], store.shape[0]
    n = b * own // q
    nb, nc = n * BS, n * CS
    vm = pltpu.VMEM
    dma = pltpu.SemaphoreType.DMA
    out = pl.pallas_call(
        functools.partial(kernel, n),
        out_shape=jax.ShapeDtypeStruct((b * own, N2), F32),
        in_specs=[
            pl.BlockSpec(memory_space=pl.ANY),
            pl.BlockSpec(memory_space=pltpu.VMEM),
            pl.BlockSpec(memory_space=pl.ANY),
            pl.BlockSpec(memory_space=pl.ANY),
        ],
        out_specs=pl.BlockSpec(memory_space=pl.ANY),
        scratch_shapes=[
            vm((n, 16 * q, K), F32),
            vm((32 * q, K), BF16),
            vm((K, N1), BF16),
            vm((K, N1), BF16),
            vm((NB, PT, N1), F32),
            vm((S1 * BS, 16 * q, N1 // BS), F32),
            vm((nb, 2, 4 * q, N1 // BS), F32),
            vm((nb, 2 * q, N1 // BS), F32),
            vm((nb, 2, 2 * q, N1 // BS), F32),
            vm((nb, 16 * q, N1 // BS), F32),
            vm((16 * q, N1), BF16),
            vm((N1, N2), BF16),
            vm((NS, 256, N1), BF16),
            vm((S2 * CS, 16 * q, N2 // CS), F32),
            vm((nc, 8 * q, N2 // CS), F32),
            vm((nc, 2, 2, q, N2 // CS), F32),
            vm((nc, q, N2 // CS), F32),
            vm((nc, 2, q, N2 // CS), F32),
            vm((b * own, N2), F32),
            dma((n,)),
            dma((n,)),
            dma((NB,)),
            dma((NS,)),
            dma((n,)),
            dma((n, 2)),
            dma((n, 2)),
            dma((n,)),
            dma((nb, 3)),
            dma((nb, 2)),
            dma((nb,)),
            dma((nb, 2)),
            dma((nb,)),
            dma((nc, 2)),
            dma((nc,)),
            dma((nc, 2)),
            dma((nc,)),
        ],
        compiler_params=pltpu.CompilerParams(
            collective_id=0, has_side_effects=True, vmem_limit_bytes=63 * 1024 * 1024
        ),
        cost_estimate=pl.CostEstimate(flops=2 * 16 * b * own * (3 * K * N1 + N1 * N2), bytes_accessed=24 << 20, transcendentals=0),
        name="scores",
    )(queries.reshape(b * own, K), column_gain, precond, store)
    return out.reshape(b, own, N2)


def solution(mesh):
    return jax.shard_map(
        local,
        mesh=mesh,
        in_specs=(P(None, "col", "row"), P("row", "col"), P("col"), P("row", "col")),
        out_specs=P(None, "col", "row"),
        check_vma=False,
    )
```

time: 115 us -> 111 us (0.965)
  Pallas kernels: 113 us -> 109 us
    pallas_call x1, Pallas kernels: 113 us -> 109 us  [local(): pl.pallas_call(functools.partial(kernel, n), out_shape=jax.ShapeDtypeStru...]
where the time goes in v4:
time: 111 us
  Pallas kernels  109 us (98%)
  local copies, waits for them, and re-layouts  1.92 us (2%)
    pallas_call x1, Pallas kernels, local(): pl.pallas_call(functools.partial(kernel, n), out_shape=jax.ShapeDtypeStru...  109 us

profile of v4, /device:TPU:1, one launch (start us, length us, event | category | flops | bytes accessed | tf_op | source)
XLA Modules:
  0.0 110.8 jit_solution(8157689004244647578)
XLA Ops:
  0.0 108.8 %scores.1 = f32[48,3072]{1,0:T(8,128)} custom-call(f32[48,2560]{1,0:T(8,128)} %bitcast.3, f32[1280]{0:T(1024)} %gain.1, f32[2560,1280]{1,0:T(8,128)} %precond.1, bf16[3072,1280]{1,0:T(8,128)(2,1)} %store.1), custom_call_target="tpu_custom_call" | custom-call | flops 21139292160 | bytes 25165824 | tf_op jit(solution)/shard_map/scores/pallas_call | solution.py:378
  108.8 1.9 %copy.6 = f32[2,24,3072]{2,1,0:T(8,128)} copy(f32[2,24,3072]{2,1,0:T(8,128)} %bitcast.2) | data formatting | bytes 1179648

commit v5 on v4

--- a/solution.py
+++ b/solution.py
@@ -16,24 +16,24 @@
 BS, CS = 2, 2
 ORDER = (
     ("A1", 0), ("PR", 0), ("A2y", 0), ("A1", 1), ("A2z", 0), ("PR", 1), ("A2y", 1), ("A2c", 0), ("A1", 2),
-    ("A3", 0), ("A2z", 1), ("A2c", 1), ("M1", 0), ("A2y", 2), ("A1", 3), ("A3", 1), ("M1", 1), ("A2z", 2),
-    ("M1", 2), ("A2c", 2), ("M1", 3), ("B1y", 1), ("B2", 1), ("A3", 2), ("B1y", 0), ("A2z", 3), ("A1", 4),
-    ("B2", 0), ("A2y", 3), ("B1y", 2), ("M1", 4), ("M1", 5), ("B3", 0), ("B2", 2), ("ST", 0), ("A2z", 4),
-    ("B1y", 3), ("A2c", 3), ("A1", 5), ("B2", 3), ("A3", 3), ("B1y", 4), ("B1y", 5), ("B3", 1), ("M1", 6),
-    ("A2y", 4), ("M1", 7), ("B3", 2), ("B5", 1), ("B2", 4), ("B3", 3), ("B2", 5), ("A2z", 5), ("B6a", 0),
-    ("B6a", 1), ("B5", 0), ("A2c", 4), ("A2y", 5), ("A3", 4), ("B1y", 6), ("ST", 1), ("A2c", 5), ("ST", 2),
-    ("M1", 8), ("B2", 6), ("B1y", 7), ("B6a", 2), ("M1", 9), ("B5", 3), ("B5", 2), ("A3", 5), ("B6a", 3),
-    ("B2", 7), ("B3", 4), ("M2", 0), ("M2", 1), ("B3", 6), ("C1", 0), ("C1", 1), ("B3", 5), ("M1", 10),
-    ("B6a", 4), ("C1y", 0), ("B5", 4), ("B1y", 8), ("B3", 7), ("B1y", 9), ("B2", 8), ("M2", 2), ("C1y", 1),
-    ("B6a", 6), ("B5", 5), ("B2", 9), ("C1", 2), ("B6a", 5), ("M2", 3), ("C2", 1), ("M1", 11), ("B5", 7),
-    ("C2", 0), ("C1y", 2), ("C1", 3), ("B3", 8), ("M2", 4), ("B6a", 7), ("B5", 6), ("M2", 5), ("B1y", 10),
-    ("B2", 10), ("C1", 4), ("C1", 5), ("B3", 9), ("B5", 8), ("B6a", 8), ("B1y", 11), ("B2", 11), ("M2", 6),
-    ("C3", 0), ("C1y", 4), ("B3", 10), ("C1y", 3), ("M2", 7), ("C1", 6), ("C1y", 5), ("B5", 9), ("B6a", 9),
-    ("C1", 7), ("B3", 11), ("C1y", 6), ("C2", 3), ("C2", 2), ("B6a", 10), ("B5", 10), ("M2", 8), ("M2", 9),
-    ("B6a", 11), ("C1y", 7), ("B5", 11), ("C1", 8), ("C1", 9), ("C3", 2), ("C2", 6), ("C2", 4), ("C2", 5),
-    ("C3", 3), ("M2", 10), ("C3", 1), ("C2", 7), ("C1y", 8), ("M2", 11), ("C1", 10), ("C3", 6), ("C1", 11),
-    ("C3", 4), ("C2", 8), ("C1y", 10), ("C1y", 9), ("C2", 10), ("C2", 9), ("C1y", 11), ("C3", 8), ("C2", 11),
-    ("C3", 10), ("C3", 7), ("C3", 9), ("C3", 5), ("C3", 11),
+    ("A3", 0), ("ST", 0), ("A2z", 1), ("M1", 0), ("A2y", 2), ("A2c", 1), ("A1", 3), ("A3", 1), ("M1", 1),
+    ("A2z", 2), ("B1y", 0), ("B2", 0), ("M1", 2), ("A2y", 3), ("B1y", 1), ("A2c", 2), ("A1", 4), ("B2", 1),
+    ("A2z", 3), ("A3", 2), ("B3", 0), ("M1", 3), ("M1", 4), ("M1", 5), ("B3", 1), ("A2y", 4), ("A1", 5),
+    ("B6a", 0), ("A2c", 3), ("ST", 1), ("A2z", 4), ("A3", 3), ("B1y", 3), ("B1y", 4), ("B2", 4), ("ST", 2),
+    ("B5", 1), ("B5", 0), ("B1y", 2), ("B1y", 5), ("B6a", 1), ("M1", 6), ("B2", 5), ("M1", 7), ("B2", 3),
+    ("B2", 2), ("M2", 0), ("A2y", 5), ("B1y", 6), ("A2z", 5), ("A2c", 5), ("B3", 5), ("B2", 6), ("A2c", 4),
+    ("A3", 4), ("B3", 4), ("M2", 1), ("B3", 2), ("C1", 0), ("B1y", 7), ("B3", 3), ("C1", 1), ("M1", 8),
+    ("B2", 7), ("A3", 5), ("B6a", 4), ("B5", 5), ("B6a", 5), ("M1", 9), ("B5", 4), ("B6a", 2), ("C1y", 0),
+    ("B5", 2), ("M1", 10), ("B5", 3), ("C1y", 1), ("B6a", 3), ("C2", 0), ("C2", 1), ("B3", 7), ("B3", 6),
+    ("B1y", 8), ("M2", 4), ("B2", 8), ("M2", 5), ("M1", 11), ("C1", 5), ("B1y", 9), ("C3", 0), ("B2", 9),
+    ("C1", 4), ("M2", 2), ("B5", 7), ("B5", 6), ("B6a", 7), ("B6a", 6), ("M2", 3), ("B1y", 10), ("B2", 10),
+    ("C1y", 5), ("C1", 2), ("B3", 9), ("B3", 8), ("B1y", 11), ("B2", 11), ("M2", 6), ("C1y", 4), ("C1", 3),
+    ("B3", 10), ("C1", 6), ("M2", 7), ("B5", 8), ("B6a", 9), ("B6a", 8), ("C1y", 2), ("B5", 9), ("C1", 7),
+    ("B3", 11), ("C1y", 3), ("C2", 3), ("C2", 2), ("C1y", 6), ("B6a", 10), ("B5", 10), ("M2", 8), ("M2", 9),
+    ("B6a", 11), ("C1y", 7), ("B5", 11), ("C1", 8), ("C2", 7), ("C2", 5), ("C2", 4), ("C1", 9), ("M2", 10),
+    ("C1y", 8), ("M2", 11), ("C2", 8), ("C1", 10), ("C1", 11), ("C3", 1), ("C3", 3), ("C2", 6), ("C1y", 10),
+    ("C1y", 9), ("C3", 4), ("C2", 10), ("C3", 7), ("C1y", 11), ("C2", 9), ("C2", 11), ("C3", 5), ("C3", 6),
+    ("C3", 9), ("C3", 8), ("C3", 2), ("C3", 10), ("C3", 11),
 )
 F32, BF16 = jnp.float32, jnp.bfloat16
 
@@ -264,6 +264,11 @@
         cols = pl.ds(h * (N2 // CS), N2 // CS)
         p2[k % (S2 * CS)] = jnp.dot(lowb[...], sv[:, cols], preferred_element_type=F32)
         c_c(k).start()
+        if h == CS - 1:
+            for part in range(b * BS, b * BS + BS):
+                went(low.at[part, pl.ds(0, 14 * q)], b_s.at[part, 2])
+                if b >= n - S1:
+                    went(p1.at[part % (S1 * BS), pl.ds(0, 10 * q)], b_s.at[part, 0])
 
     def C1(k):
         came(rc.at[k], cc_r.at[k])
@@ -356,10 +361,6 @@
             if left[k // CS] == 0:
                 o_out(k // CS).start()
 
-    for k in range(n * BS):
-        went(low.at[k, pl.ds(0, 14 * q)], b_s.at[k, 2])
-        if k >= (n - S1) * BS:
-            went(p1.at[k % (S1 * BS), pl.ds(0, 10 * q)], b_s.at[k, 0])
     for k in range(n):
         o_out(k).wait()
     for k in range(n * CS):

time: 111 us -> 111 us (level)
  no operation moved by 1% of the time
where the time goes in v5:
time: 111 us
  Pallas kernels  109 us (98%)
  local copies, waits for them, and re-layouts  1.92 us (2%)
    pallas_call x1, Pallas kernels, local(): pl.pallas_call(functools.partial(kernel, n), out_shape=jax.ShapeDtypeStru...  109 us

profile of v5, /device:TPU:1, one launch (start us, length us, event | category | flops | bytes accessed | tf_op | source)
XLA Modules:
  0.0 110.8 jit_solution(9514785636268523651)
XLA Ops:
  0.0 108.9 %scores.1 = f32[48,3072]{1,0:T(8,128)} custom-call(f32[48,2560]{1,0:T(8,128)} %bitcast.3, f32[1280]{0:T(1024)} %gain.1, f32[2560,1280]{1,0:T(8,128)} %precond.1, bf16[3072,1280]{1,0:T(8,128)(2,1)} %store.1), custom_call_target="tpu_custom_call" | custom-call | flops 21139292160 | bytes 25165824 | tf_op jit(solution)/shard_map/scores/pallas_call | solution.py:379
  108.9 1.9 %copy.6 = f32[2,24,3072]{2,1,0:T(8,128)} copy(f32[2,24,3072]{2,1,0:T(8,128)} %bitcast.2) | data formatting | bytes 1179648
